TPU v7x, 32 devices: a whole 2x2x4 slice. The times are simulated.
32 devices in a mesh: grp: 2 (over y), pts: 8 (over z, x), ctr: 2 (over core).
Axes of the slice: x: 2, y: 2, z: 4, core: 2. Of those that a mesh axis runs over, the one named last changes fastest.
Arguments:
- points: bfloat16 [3072, 128], P(('grp', 'pts')), parts along dimension 0, may hold values from -1.5 to 1.5
- curvature: bfloat16 [3072, 32], P(('grp', 'pts')), parts along dimension 0, may hold values from 0.019897461 to 0.25
- centers: bfloat16 [128, 131072], P(None, ('grp', 'pts', 'ctr')), parts along dimension 1, may hold values from -1.5 to 1.5
- coef: bfloat16 [32, 131072], P(None, ('grp', 'pts', 'ctr')), parts along dimension 1, may hold values from -1.1953125 to 1.1953125
Outputs:
- hvp: float32 [32, 131072], P(None, ('grp', 'pts', 'ctr')), parts along dimension 1
There are 2 independent parts, one for each index of `grp`. A program takes and returns all parts, laid end to end along the dimension named above; each array names one. Nothing has to cross between parts.
All inputs are finite; a program needn't handle non-finite values.
Results may differ from a plain program's by a relative error of at most 0.0003.
Values may be sent and summed in bfloat16 or wider, within the bound.
A program may use at most 64 MiB of HBM per device.

v0:
```python
import jax
import jax.numpy as jnp
from jax import lax
from jax.sharding import PartitionSpec as P


def kernel_tile(points, sq_points, block, scale):
    sq_centers = jnp.sum(jnp.square(block.astype(jnp.float32)), axis=0)
    inner = jnp.dot(points, block, preferred_element_type=jnp.float32)
    dist = sq_points[:, None] + sq_centers[None, :] - 2.0 * inner
    return jnp.exp(-dist * scale).astype(jnp.bfloat16)


def on_device(points, curvature, centers, coef):
    scale = 32.0 / points.shape[1]
    labels = coef.shape[0]
    near_centers, near_coef = (
        lax.all_gather(centers, "pts", axis=1, tiled=True),
        lax.all_gather(coef, "pts", axis=1, tiled=True),
    )
    total = near_centers.shape[1]
    width = total // 4
    sq_points = jnp.sum(jnp.square(points.astype(jnp.float32)), axis=1)
    tangent = jnp.zeros((points.shape[0], labels), jnp.float32)
    for number in range(4):
        block = near_centers[:, number * width : (number + 1) * width]
        tile = kernel_tile(points, sq_points, block, scale)
        values = near_coef[:, number * width : (number + 1) * width]
        tangent = tangent + lax.dot_general(
            tile, values, (((1,), (1,)), ((), ())), preferred_element_type=jnp.float32
        )
    tangent = lax.psum(tangent, "ctr")
    weighted = (curvature.astype(jnp.float32) * tangent).astype(jnp.bfloat16)
    pieces = []
    for number in range(4):
        block = near_centers[:, number * width : (number + 1) * width]
        tile = kernel_tile(points, sq_points, block, scale)
        pieces.append(
            lax.dot_general(
                weighted, tile, (((0,), (0,)), ((), ())), preferred_element_type=jnp.float32
            )
        )
    partial_sum = jnp.concatenate(pieces, axis=1)
    return lax.psum_scatter(partial_sum, "pts", scatter_dimension=1, tiled=True)


def solution(mesh):
    in_specs = (
        P(("grp", "pts"), None),
        P(("grp", "pts"), None),
        P(None, ("grp", "pts", "ctr")),
        P(None, ("grp", "pts", "ctr")),
    )
    out_specs = P(None, ("grp", "pts", "ctr"))
    return jax.shard_map(
        on_device, mesh=mesh, in_specs=in_specs, out_specs=out_specs, check_vma=False
    )
```

profile of v0, /device:TPU:1, one launch (start us, length us, event | category | flops | bytes accessed | tf_op | source)
XLA Modules:
  0.0 298.4 jit_solution(7907585057710424661)
XLA Ops:
  6.5 0.7 all-gather.3.cloned.1.call-update
  7.3 0.7 all-gather.5.cloned.1.call-update
  8.1 0.9 multiply_reduce_fusion.4
  9.0 127.2 %all-gather.3.cloned.1.call-done = bf16[128,32768]{1,0:T(8,128)(2,1)} async-done(((bf16[128,4096]{1,0:T(8,128)(2,1)}), bf16[128,32768]{1,0:T(8,128)(2,1)}) %all-gather.3.cloned.1.call-update) | async-done | bytes 8388624 | tf_op jit(solution)/shard_map/all_gather | solution.py:18
  136.2 4.5 %multiply_reduce_fusion = (f32[8192]{0:T(1024)S(1)}, f32[8192]{0:T(1024)S(1)}, f32[8192]{0:T(1024)S(1)}, f32[8192]{0:T(1024)S(1)}) fusion(bf16[128,32768]{1,0:T(8,128)(2,1)} %all-gather.3.cloned.1.call-done), kind=kLoop, calls=%fused_computation.25 | loop fusion | flops 12550144 | bytes 8519680 | tf_op jit(solution)/shard_map/reduce_sum | solution.py:8
  140.7 1.3 copy-done.4
  142.0 1.8 fusion.19
  143.8 3.5 %fusion.18 = bf16[192,8192]{1,0:T(8,128)(2,1)} fusion(bf16[192,128]{1,0:T(8,128)(2,1)S(1)} %copy-done.6, f32[8192]{0:T(1024)S(1)} %get-tuple-element.6, f32[192]{0:T(256)S(1)} %multiply_reduce_fusion.4, bf16[128,32768]{1,0:T(8,128)(2,1)S(1)} %copy-done.4), kind=kOutput, calls=%fused_computation.22 | convolution fusion | flops 412090368 | bytes 5325824 | tf_op jit(solution)/shard_map/dot_general | solution.py:9
  147.4 3.5 %fusion.17 = bf16[192,8192]{1,0:T(8,128)(2,1)} fusion(bf16[192,128]{1,0:T(8,128)(2,1)S(1)} %copy-done.6, f32[8192]{0:T(1024)S(1)} %get-tuple-element.7, f32[192]{0:T(256)S(1)} %multiply_reduce_fusion.4, bf16[128,32768]{1,0:T(8,128)(2,1)S(1)} %copy-done.4), kind=kOutput, calls=%fused_computation.21 | convolution fusion | flops 412090368 | bytes 5325824 | tf_op jit(solution)/shard_map/dot_general | solution.py:9
  150.9 3.5 %fusion.16 = bf16[192,8192]{1,0:T(8,128)(2,1)} fusion(bf16[192,128]{1,0:T(8,128)(2,1)S(1)} %copy-done.6, f32[8192]{0:T(1024)S(1)} %get-tuple-element.8, f32[192]{0:T(256)S(1)} %multiply_reduce_fusion.4, bf16[128,32768]{1,0:T(8,128)(2,1)S(1)} %copy-done.4), kind=kOutput, calls=%fused_computation.20 | convolution fusion | flops 412090368 | bytes 5325824 | tf_op jit(solution)/shard_map/dot_general | solution.py:9
  154.4 30.7 %all-gather.5.cloned.1.call-done = bf16[32,32768]{1,0:T(8,128)(2,1)} async-done(((bf16[32,4096]{1,0:T(8,128)(2,1)}), bf16[32,32768]{1,0:T(8,128)(2,1)}) %all-gather.5.cloned.1.call-update) | async-done | bytes 2097168 | tf_op jit(solution)/shard_map/all_gather | solution.py:19
  185.1 3.2 %fusion.27 = f32[192,32]{0,1:T(8,128)S(1)} fusion(bf16[192,8192]{1,0:T(8,128)(2,1)} %fusion.16, bf16[32,32768]{1,0:T(8,128)(2,1)} %all-gather.5.cloned.1.call-done), kind=kOutput, calls=%fused_computation.39 | convolution fusion | flops 100663296 | bytes 3694592 | tf_op jit(solution)/shard_map/dot_general | solution.py:29
  188.4 3.1 %convolution_add_fusion.2 = f32[192,32]{0,1:T(8,128)S(1)} fusion(f32[192,32]{0,1:T(8,128)S(1)} %fusion.27, bf16[192,8192]{1,0:T(8,128)(2,1)} %fusion.17, bf16[32,32768]{1,0:T(8,128)(2,1)} %all-gather.5.cloned.1.call-done), kind=kOutput, calls=%fused_computation.35 | convolution fusion | flops 100669440 | bytes 3719168 | tf_op jit(solution)/shard_map/dot_general | solution.py:29
  191.5 1.1 convolution_add_fusion.1
  192.5 1.1 convolution_add_fusion
  193.6 5.0 %psum.7 = f32[192,32]{0,1:T(8,128)S(1)} all-reduce(f32[192,32]{0,1:T(8,128)S(1)} %convolution_add_fusion), channel_id=1, replica_groups=mesh['grp'=2,'pts'=8,'ctr'=2] {'ctr'}, use_global_device_ids=true, to_apply=%region_5.0 | all-reduce | flops 6144 | bytes 49152 | tf_op jit(solution)/shard_map/psum | solution.py:32
  198.7 0.7 fusion.32
  199.4 1.2 copy-done.1
  200.6 0.7 fusion.31
  201.5 0.7 fusion.30
  202.2 0.5 copy-done.3
  202.7 0.7 fusion.29
  203.3 2.2 pad_maximum_fusion
  205.6 86.3 %reduce-scatter.2.cloned.1.call-done = f32[32,4096]{1,0:T(8,128)} async-done(((f32[32,32768]{1,0:T(8,128)}), f32[32,4096]{1,0:T(8,128)}) %reduce-scatter.2.cloned.1.call-update) | async-done | bytes 524304 | tf_op jit(solution)/shard_map/reduce_scatter | solution.py:44
  (18 shorter events, 0.4 us)
Async XLA Ops:
  6.5 129.6 %all-gather.3.cloned.1.call-start = ((), (), s32[]{:S(2)}) async-start(), calls=%async_computation.1 | async-start | bytes 9437184 | tf_op jit(solution)/shard_map/all_gather | solution.py:18
  7.3 177.9 %all-gather.5.cloned.1.call-start = ((), (), s32[]{:S(2)}) async-start(), calls=%async_computation.2 | async-start | bytes 2359296 | tf_op jit(solution)/shard_map/all_gather | solution.py:19
  8.0 283.9 %reduce-scatter.2.cloned.1.call-start = ((), (), s32[]{:S(2)}) async-start(), calls=%async_computation.3 | async-start | bytes 4718592 | tf_op jit(solution)/shard_map/reduce_scatter | solution.py:44
  9.0 131.7 %copy-start.6 = (bf16[192,128]{1,0:T(8,128)(2,1)S(1)}, bf16[192,128]{1,0:T(8,128)(2,1)}, u32[]{:S(2)}) copy-start(bf16[192,128]{1,0:T(8,128)(2,1)} %param.4) | copy-start | bytes 147460
  136.2 5.9 %copy-start.4 = (bf16[128,32768]{1,0:T(8,128)(2,1)S(1)}, bf16[128,32768]{1,0:T(8,128)(2,1)}, u32[]{:S(2)}) copy-start(bf16[128,32768]{1,0:T(8,128)(2,1)} %all-gather.3.cloned.1.call-done) | copy-start | bytes 25165828
  185.1 6.3 %copy-start = (bf16[192,8192]{1,0:T(8,128)(2,1)S(1)}, bf16[192,8192]{1,0:T(8,128)(2,1)}, u32[]{:S(2)}) copy-start(bf16[192,8192]{1,0:T(8,128)(2,1)} %fusion.18) | copy-start | bytes 9437188
  185.1 6.3 %copy-start.5 = (bf16[32,32768]{1,0:T(8,128)(2,1)S(1)}, bf16[32,32768]{1,0:T(8,128)(2,1)}, u32[]{:S(2)}) copy-start(bf16[32,32768]{1,0:T(8,128)(2,1)} %all-gather.5.cloned.1.call-done) | copy-start | bytes 6291460
  191.4 7.2 %copy-start.7 = (bf16[192,32]{0,1:T(8,128)(2,1)S(1)}, bf16[192,32]{0,1:T(8,128)(2,1)}, u32[]{:S(2)}) copy-start(bf16[192,32]{0,1:T(8,128)(2,1)} %param.5) | copy-start | bytes 36868
  198.7 1.9 copy-start.1
  198.7 2.8 copy-start.2
  200.5 2.1 copy-start.3
Sparse Core Ops, SparseCore 0:
  9.5 126.5 all-gather.2
  138.3 46.7 all-gather.4
  205.7 86.1 reduce-scatter.1
where the time goes:
time: 299 us; the launch traced here: 298 us
  waiting for transfers between devices  246 us (82%)
  matrix products  23.5 us (8%)
  between operations  13.2 us (4%)
  other arithmetic  7.63 us (3%)
  blocking collectives  5.02 us (2%)
  local copies, waits for them, and re-layouts  3.28 us (1%)
    all_gather x1, waiting for transfers between devices, on_device(): lax.all_gather(centers, 'pts', axis=1, tiled=True)  127 us
    reduce_scatter x1, waiting for transfers between devices, on_device(): return lax.psum_scatter(partial_sum, 'pts', scatter_dimension=1, tiled=True)  86.3 us
    all_gather x1, waiting for transfers between devices, on_device(): lax.all_gather(coef, 'pts', axis=1, tiled=True)  30.7 us
    dot_general x4, matrix products, kernel_tile(): inner = jnp.dot(points, block, preferred_element_type=jnp.float32)  12.4 us
    dot_general x4, matrix products, on_device(): lax.dot_general(tile, values, (((1,), (1,)), ((), ())), preferred_element...  8.43 us
  transfers between devices with their start and end apart: 3, of which 3 were waited for; matrix products, arithmetic and copies ran while one was open for 6% of the time, Pallas kernels for 0%

commit v1 on v0

v1 whole, which is shorter than its diff:
```python
import functools
import math

import jax
import jax.numpy as jnp
from jax import lax
from jax.experimental import pallas as pl
from jax.experimental.pallas import tpu as pltpu
from jax.sharding import PartitionSpec as P

MESH = pl.DeviceIdType.MESH
F32, BF16 = jnp.float32, jnp.bfloat16
NT = (((1,), (1,)), ((), ()))


def xor(a, b, size):
    both, bit = 0, 1
    while bit < size:
        both = both + ((a // bit) % 2) * ((b // bit) % 2) * bit
        bit *= 2
    return a + b - 2 * both


def split3(x):
    high = x.astype(BF16).astype(F32)
    rest = x - high
    middle = rest.astype(BF16).astype(F32)
    low = (rest - middle).astype(BF16).astype(F32)
    return high, middle, low


def kernel(n, m, factor, points, curvature, centers, coef, out,
           near, tile, aug, part, got, weight, curve,
           p_send, p_recv, t_send, t_recv, w_send, w_recv):
    j, c = lax.axis_index("pts"), lax.axis_index("ctr")
    rows, depth = points.shape
    total = centers.shape[1]
    labels = coef.shape[0]
    count = n * m
    me = j * m + c
    wide = min(512, total)

    def place(t):
        other = xor(me, t, count)
        return {"pts": other // m, "ctr": other % m}

    barrier = pltpu.get_barrier_semaphore()

    def greet(t, carry):
        pl.semaphore_signal(barrier, inc=1, device_id=place(t), device_id_type=MESH)
        return carry

    lax.fori_loop(1, count, greet, 0)
    pl.semaphore_wait(barrier, count - 1)

    def point_copy(s):
        return pltpu.make_async_remote_copy(
            src_ref=points, dst_ref=near.at[j],
            send_sem=p_send.at[s], recv_sem=p_recv.at[s],
            device_id={"pts": xor(j, s, n)}, device_id_type=MESH,
        )

    def send_points(s, carry):
        point_copy(s).start()
        return carry

    lax.fori_loop(1, n, send_points, 0)

    def augment():
        block = centers[...].astype(F32)
        high, middle, low = split3(-0.5 * jnp.sum(block * block, axis=0, keepdims=True))
        spot = lax.broadcasted_iota(jnp.int32, (depth, total), 0)
        extra = jnp.where(spot < 6, 1.0, 0.0)
        for number, value in enumerate((high, middle, low)):
            extra = jnp.where(spot == number, value, extra)
        aug[0:depth, :] = centers[...]
        aug[depth : 2 * depth, :] = extra.astype(BF16)
        turned = curvature[...].astype(F32)
        for number in range(m):
            curve[number] = turned[number * (labels // m) : (number + 1) * (labels // m), :]

    augment()

    def pair(block, b):
        wider = block.astype(F32)
        high, middle, low = split3(-0.5 * jnp.sum(wider * wider, axis=1, keepdims=True))
        spot = lax.broadcasted_iota(jnp.int32, (rows, depth), 1)
        extra = jnp.where(spot < 3, 1.0, 0.0)
        for number, value in enumerate((high, middle, low)):
            extra = jnp.where(spot == number + 3, value, extra)
        left = jnp.concatenate([block, extra.astype(BF16)], axis=1)
        for start in range(0, total, wide):
            inner = jnp.dot(left, aug[:, start : start + wide], preferred_element_type=F32)
            tile[b, :, start : start + wide] = jnp.exp2(inner * factor).astype(BF16)
        value = lax.dot_general(coef[...], tile[b], NT, preferred_element_type=F32)
        for number in range(m):
            part[b, number] = value[number * (labels // m) : (number + 1) * (labels // m), :]

    def part_copy(s, d):
        t = s * m + d
        b, cc = xor(j, s, n), xor(c, d, m)
        return pltpu.make_async_remote_copy(
            src_ref=part.at[b, cc], dst_ref=got.at[t],
            send_sem=t_send.at[t], recv_sem=t_recv.at[t],
            device_id={"pts": b, "ctr": cc}, device_id_type=MESH,
        )

    pair(points[...], j)
    got[0] = part[j, c]
    for d in range(1, m):
        part_copy(0, d).start()

    def step(s, carry):
        b = xor(j, s, n)
        point_copy(s).wait_recv()
        pair(near[b], b)
        for d in range(m):
            part_copy(s, d).start()
        return carry

    lax.fori_loop(1, n, step, 0)

    def arrived(t, value):
        part_copy(t // m, t % m).wait_recv()
        return value + got[t]

    value = lax.fori_loop(1, count, arrived, got[0])
    weight[j, c] = (curve[c] * value).astype(BF16)

    def weight_copy(t):
        return pltpu.make_async_remote_copy(
            src_ref=weight.at[j, c], dst_ref=weight.at[j, c],
            send_sem=w_send.at[t], recv_sem=w_recv.at[t],
            device_id=place(t), device_id_type=MESH,
        )

    def send_weight(t, carry):
        weight_copy(t).start()
        return carry

    lax.fori_loop(1, count, send_weight, 0)

    def wait_weight(t, carry):
        weight_copy(t).wait_recv()
        return carry

    lax.fori_loop(1, count, wait_weight, 0)

    def project(i, carry):
        columns = pl.ds(pl.multiple_of(i * wide, wide), wide)

        def add(b, value):
            left = jnp.concatenate([weight[b, number] for number in range(m)], axis=0)
            return value + jnp.dot(left, tile[b, :, columns], preferred_element_type=F32)

        value = jnp.zeros((labels, wide), F32)
        if n <= 16:
            for b in range(n):
                value = add(b, value)
        else:
            value = lax.fori_loop(0, n, add, value)
        out[:, columns] = value
        return carry

    lax.fori_loop(0, total // wide, project, 0)

    def finish(t, carry):
        part_copy(t // m, t % m).wait_send()
        weight_copy(t).wait_send()
        return carry

    lax.fori_loop(1, count, finish, 0)

    def finish_points(s, carry):
        point_copy(s).wait_send()
        return carry

    lax.fori_loop(1, n, finish_points, 0)


def solution(mesh):
    n, m = mesh.shape["pts"], mesh.shape["ctr"]

    def on_device(points, curvature, centers, coef):
        rows, depth = points.shape
        labels, total = coef.shape
        factor = 2.0 * (32.0 / depth) * math.log2(math.e)
        share = labels // m
        return pl.pallas_call(
            functools.partial(kernel, n, m, factor),
            out_shape=jax.ShapeDtypeStruct((labels, total), F32),
            in_specs=[pl.BlockSpec(memory_space=pltpu.VMEM)] * 4,
            out_specs=pl.BlockSpec(memory_space=pltpu.VMEM),
            scratch_shapes=[
                pltpu.VMEM((n, rows, depth), BF16),
                pltpu.VMEM((n, rows, total), BF16),
                pltpu.VMEM((2 * depth, total), BF16),
                pltpu.VMEM((n, m, share, rows), F32),
                pltpu.VMEM((n * m, share, rows), F32),
                pltpu.VMEM((n, m, share, rows), BF16),
                pltpu.VMEM((m, share, rows), F32),
                pltpu.SemaphoreType.DMA((n,)),
                pltpu.SemaphoreType.DMA((n,)),
                pltpu.SemaphoreType.DMA((n * m,)),
                pltpu.SemaphoreType.DMA((n * m,)),
                pltpu.SemaphoreType.DMA((n * m,)),
                pltpu.SemaphoreType.DMA((n * m,)),
            ],
            compiler_params=pltpu.CompilerParams(
                collective_id=0, has_side_effects=True, vmem_limit_bytes=56 << 20
            ),
        )(points, curvature.T, centers, coef)

    in_specs = (
        P(("grp", "pts"), None),
        P(("grp", "pts"), None),
        P(None, ("grp", "pts", "ctr")),
        P(None, ("grp", "pts", "ctr")),
    )
    out_specs = P(None, ("grp", "pts", "ctr"))
    return jax.shard_map(
        on_device, mesh=mesh, in_specs=in_specs, out_specs=out_specs, check_vma=False
    )
```

time: 299 us -> 35.7 us (0.12)
  waiting for transfers between devices: 246 us -> 0 us
  Pallas kernels: 0 us -> 33.3 us
  matrix products: 23.5 us -> 0 us
  between operations: 13.2 us -> 0.01 us
  other arithmetic: 7.63 us -> 0 us
  blocking collectives: 5.02 us -> 0 us
    all_gather x2 -> x0, waiting for transfers between devices: 158 us -> none  [the longest x1 127 us: on_device(): lax.all_gather(centers, 'pts', axis=1, tiled=True)]
    reduce_scatter x1 -> x0, waiting for transfers between devices: 86.3 us -> none  [on_device(): return lax.psum_scatter(partial_sum, 'pts', scatter_dimension=1, tiled=True)]
    pallas_call x0 -> x1, Pallas kernels: none -> 33.3 us  [on_device(): pl.pallas_call(functools.partial(kernel, n, m, factor), out_shape=jax.Sha...]
    dot_general x12 -> x0, matrix products: 23.5 us -> none  [the longest x4 12.4 us: kernel_tile(): inner = jnp.dot(points, block, preferred_element_type=jnp.float32)]
    reduce_sum x2 -> x0, other arithmetic: 5.41 us -> none  [the longest x1 4.5 us: kernel_tile(): sq_centers = jnp.sum(jnp.square(block.astype(jnp.float32)), axis=0)]
    psum x1 -> x0, blocking collectives: 5.02 us -> none  [on_device(): tangent = lax.psum(tangent, 'ctr')]
  transfers between devices with their start and end apart: 3 -> 0, of which waited for: 3 -> 0; matrix products, arithmetic and copies ran while one was open for 6% -> 0% of each run, Pallas kernels for 0% -> 0%
where the time goes in v1:
time: 35.7 us; the launch traced here: 35.1 us
  Pallas kernels  33.3 us (93%)
  local copies, waits for them, and re-layouts  1.87 us (5%)
    pallas_call x1, Pallas kernels, on_device(): pl.pallas_call(functools.partial(kernel, n, m, factor), out_shape=jax.Sha...  33.3 us
    unnamed x1, local copies, waits for them, and re-layouts  1.87 us

profile of v1, /device:TPU:1, one launch (start us, length us, event | category | flops | bytes accessed | tf_op | source)
XLA Modules:
  0.0 35.1 jit_solution(9277884995130745612)
XLA Ops:
  0.0 33.3 %shard_map.46 = f32[32,4096]{1,0:T(8,128)} custom-call(bf16[192,128]{1,0:T(8,128)(2,1)} %points.1, bf16[32,192]{1,0:T(8,128)(2,1)} %bitcast.1, bf16[128,4096]{1,0:T(8,128)(2,1)} %centers.1, bf16[32,4096]{1,0:T(8,128)(2,1)} %coef.1), custom_call_target="tpu_custom_call" | custom-call | tf_op jit(solution)/shard_map/pallas_call | solution.py:189
  33.3 1.9 %copy.6 = f32[32,4096]{1,0:T(8,128)} copy(f32[32,4096]{1,0:T(8,128)} %shard_map.46) | data formatting | bytes 1048576

commit v2 on v0

v2 whole, which is shorter than its diff:
```python
import functools
import math

import jax
import jax.numpy as jnp
from jax import lax
from jax.experimental import pallas as pl
from jax.experimental.pallas import tpu as pltpu
from jax.sharding import PartitionSpec as P

MESH = pl.DeviceIdType.MESH
F32, BF16 = jnp.float32, jnp.bfloat16


def xor(a, b, size):
    both, bit = 0, 1
    while bit < size:
        both = both + ((a // bit) % 2) * ((b // bit) % 2) * bit
        bit *= 2
    return a + b - 2 * both


def split3(x):
    high = x.astype(BF16).astype(F32)
    rest = x - high
    middle = rest.astype(BF16).astype(F32)
    low = (rest - middle).astype(BF16).astype(F32)
    return high, middle, low


def kernel(n, factor, points_in, curvature_in, centers_in, coef_in, out,
           points, curvature, centers, coef, near, tile, aug, centers2, coef2, turned, part, got, weight, mine, ours, theirs,
           p_send, p_recv, t_send, t_recv, w_send, w_recv, c_send, c_recv, o_send, o_recv, l_in, l_out):
    j, c = lax.axis_index("pts"), lax.axis_index("ctr")
    half, depth = points.shape[0] // 2, points.shape[1]
    labels, total = coef.shape
    wide = mine.shape[2]
    chunks = total // wide
    pairs = n // 2
    sibling = {"ctr": 1 - c}

    def peer(s):
        return {"pts": xor(j, s, n)}

    barrier = pltpu.get_barrier_semaphore()
    pl.semaphore_signal(barrier, inc=1, device_id=sibling, device_id_type=MESH)

    def greet(s, carry):
        pl.semaphore_signal(barrier, inc=1, device_id=peer(s), device_id_type=MESH)
        return carry

    lax.fori_loop(1, n, greet, 0)

    loads = [
        pltpu.make_async_copy(source, target, l_in.at[number])
        for number, (source, target) in enumerate(
            ((points_in, points), (centers_in, centers), (coef_in, coef), (curvature_in, curvature))
        )
    ]
    for load in loads:
        load.start()

    def augment(side, source, values):
        turned[side] = values[...].astype(F32).T.astype(BF16)
        block = source[...].astype(F32)
        high, middle, low = split3(-0.5 * jnp.sum(block * block, axis=0, keepdims=True))
        spot = lax.broadcasted_iota(jnp.int32, (depth, total), 0)
        extra = jnp.where(spot < 6, 1.0, 0.0)
        for number, value in enumerate((high, middle, low)):
            extra = jnp.where(spot == number, value, extra)
        aug[side, 0:depth, :] = source[...]
        aug[side, depth : 2 * depth, :] = extra.astype(BF16)

    own = pl.ds(pl.multiple_of(c * half, half), half)
    for load in loads:
        load.wait()
    near[0:half, :] = points[own, :]
    pl.semaphore_wait(barrier, n)

    def copy(source, target, send, receive, device):
        return pltpu.make_async_remote_copy(
            src_ref=source, dst_ref=target, send_sem=send, recv_sem=receive,
            device_id=device, device_id_type=MESH,
        )

    def point_copy(s):
        slot = pl.ds(pl.multiple_of(s * half, half), half)
        return copy(near.at[pl.ds(0, half)], near.at[slot], p_send.at[s], p_recv.at[s], peer(s))

    def each(first, last, act):
        def body(s, carry):
            act(s)
            return carry

        lax.fori_loop(first, last, body, 0)

    center_copy = copy(centers, centers2, c_send.at[0], c_recv.at[0], sibling)
    coef_copy = copy(coef, coef2, c_send.at[1], c_recv.at[1], sibling)
    point_copy(1).start()
    center_copy.start()
    coef_copy.start()

    def turn(i):
        later = i + pairs // 2 - 1
        return later - (later // pairs) * (pairs - 1)

    def send_points(i):
        point_copy(2 * turn(i)).start()
        point_copy(2 * turn(i) + 1).start()

    each(1, pairs, send_points)
    augment(0, centers, coef)

    def part_copy(s):
        return copy(part.at[s], got.at[s], t_send.at[s], t_recv.at[s], peer(s))

    def left_side(i):
        block = near[pl.ds(pl.multiple_of(i * 2 * half, 2 * half), 2 * half), :]
        wider = block.astype(F32)
        high, middle, low = split3(-0.5 * jnp.sum(wider * wider, axis=1, keepdims=True))
        spot = lax.broadcasted_iota(jnp.int32, (2 * half, depth), 1)
        extra = jnp.where(spot < 3, 1.0, 0.0)
        for number, value in enumerate((high, middle, low)):
            extra = jnp.where(spot == number + 3, value, extra)
        return jnp.concatenate([block, extra.astype(BF16)], axis=1)

    def pair(i, left, side):
        for start in range(0, total, wide):
            inner = jnp.dot(
                left, aug[side, :, start : start + wide], preferred_element_type=F32
            )
            tile[i, side, :, start : start + wide] = jnp.exp2(inner * factor).astype(BF16)
        return jnp.dot(tile[i, side], turned[side], preferred_element_type=F32)

    def keep(i, value):
        value = value.T
        part[2 * i] = value[:, 0:half]
        part[2 * i + 1] = value[:, half : 2 * half]

    point_copy(1).wait_recv()
    left = left_side(0)
    value = pair(0, left, 0)
    center_copy.wait_recv()
    coef_copy.wait_recv()
    augment(1, centers2, coef2)
    keep(0, value + pair(0, left, 1))
    part_copy(1).start()
    got[0] = part[0]

    def step(number):
        i = turn(number)
        point_copy(2 * i).wait_recv()
        point_copy(2 * i + 1).wait_recv()
        left = left_side(i)
        keep(i, pair(i, left, 0) + pair(i, left, 1))
        part_copy(2 * i).start()
        part_copy(2 * i + 1).start()

    each(1, pairs, step)

    def arrived(s, value):
        part_copy(s).wait_recv()
        return value + got[s]

    value = lax.fori_loop(1, n, arrived, got[0])
    saved = jnp.where(c == 0, curvature[:, 0:half].astype(F32), curvature[:, half : 2 * half].astype(F32))
    weight[0] = (saved * value).astype(BF16)

    def weight_copy(s):
        return copy(weight.at[0], weight.at[s], w_send.at[s], w_recv.at[s], peer(s))

    each(1, n, lambda s: weight_copy(n - s).start())

    def columns(number):
        return pl.ds(pl.multiple_of(number * wide, wide), wide)

    def join(i):
        return jnp.concatenate([weight[2 * i], weight[2 * i + 1]], axis=1)

    def project(left, i, side, number):
        return jnp.dot(left, tile[i, side, :, columns(number)], preferred_element_type=F32)

    def share_copy(number):
        return copy(mine.at[number], theirs.at[number], o_send.at[number], o_recv.at[number], sibling)

    def out_copy(number):
        return pltpu.make_async_copy(ours.at[number], out.at[:, columns(number)], l_out.at[number])

    weight_copy(1).wait_recv()
    left = join(0)

    def begin(number):
        mine[number] = project(left, 0, 1, number)
        ours[number] = project(left, 0, 0, number)

    each(0, chunks, begin)

    def middle(i):
        weight_copy(2 * i).wait_recv()
        weight_copy(2 * i + 1).wait_recv()
        left = join(i)

        def more(number):
            mine[number] += project(left, i, 1, number)
            ours[number] += project(left, i, 0, number)

        each(0, chunks, more)

    each(1, pairs - 1, middle)
    last = pairs - 1
    weight_copy(2 * last).wait_recv()
    weight_copy(2 * last + 1).wait_recv()
    left_last = join(last)

    def give(number):
        mine[number] += project(left_last, last, 1, number)
        share_copy(number).start()

    def take(number):
        value = ours[number] + project(left_last, last, 0, number)
        share_copy(number).wait_recv()
        ours[number] = value + theirs[number]
        out_copy(number).start()

    each(0, chunks, give)
    each(0, chunks, take)

    def finish(s):
        point_copy(s).wait_send()
        part_copy(s).wait_send()
        weight_copy(s).wait_send()

    each(1, n, finish)
    center_copy.wait_send()
    coef_copy.wait_send()
    each(0, chunks, lambda number: share_copy(number).wait_send())
    each(0, chunks, lambda number: out_copy(number).wait())


def solution(mesh):
    n = mesh.shape["pts"]

    def on_device(points, curvature, centers, coef):
        rows, depth = points.shape
        labels, total = coef.shape
        factor = 2.0 * (32.0 / depth) * math.log2(math.e)
        half = rows // 2
        wide = min(512, total)
        dma = pltpu.SemaphoreType.DMA
        return pl.pallas_call(
            functools.partial(kernel, n, factor),
            out_shape=jax.ShapeDtypeStruct((labels, total), F32),
            in_specs=[pl.BlockSpec(memory_space=pltpu.HBM)] * 4,
            out_specs=pl.BlockSpec(memory_space=pltpu.HBM),
            scratch_shapes=[
                pltpu.VMEM((rows, depth), BF16),
                pltpu.VMEM((labels, rows), BF16),
                pltpu.VMEM((depth, total), BF16),
                pltpu.VMEM((labels, total), BF16),
                pltpu.VMEM((n * half, depth), BF16),
                pltpu.VMEM((n // 2, 2, rows, total), BF16),
                pltpu.VMEM((2, 2 * depth, total), BF16),
                pltpu.VMEM((depth, total), BF16),
                pltpu.VMEM((labels, total), BF16),
                pltpu.VMEM((2, total, labels), BF16),
                pltpu.VMEM((n, labels, half), F32),
                pltpu.VMEM((n, labels, half), F32),
                pltpu.VMEM((n, labels, half), BF16),
                pltpu.VMEM((total // wide, labels, wide), F32),
                pltpu.VMEM((total // wide, labels, wide), F32),
                pltpu.VMEM((total // wide, labels, wide), F32),
                dma((n,)), dma((n,)), dma((n,)), dma((n,)), dma((n,)), dma((n,)),
                dma((2,)), dma((2,)), dma((total // wide,)), dma((total // wide,)),
                dma((4,)), dma((total // wide,)),
            ],
            compiler_params=pltpu.CompilerParams(
                collective_id=0, has_side_effects=True, vmem_limit_bytes=56 << 20
            ),
        )(points, curvature.T, centers, coef)

    in_specs = (
        P(("grp", "pts"), None),
        P(("grp", "pts"), None),
        P(None, ("grp", "pts", "ctr")),
        P(None, ("grp", "pts", "ctr")),
    )
    out_specs = P(None, ("grp", "pts", "ctr"))
    return jax.shard_map(
        on_device, mesh=mesh, in_specs=in_specs, out_specs=out_specs, check_vma=False
    )
```

time: 299 us -> 33.4 us (0.11)
  waiting for transfers between devices: 246 us -> 0 us
  Pallas kernels: 0 us -> 30.9 us
  matrix products: 23.5 us -> 0 us
  between operations: 13.2 us -> 0.01 us
  other arithmetic: 7.63 us -> 0 us
  blocking collectives: 5.02 us -> 0 us
    all_gather x2 -> x0, waiting for transfers between devices: 158 us -> none  [the longest x1 127 us: on_device(): lax.all_gather(centers, 'pts', axis=1, tiled=True)]
    reduce_scatter x1 -> x0, waiting for transfers between devices: 86.3 us -> none  [on_device(): return lax.psum_scatter(partial_sum, 'pts', scatter_dimension=1, tiled=True)]
    pallas_call x0 -> x1, Pallas kernels: none -> 30.9 us  [on_device(): pl.pallas_call(functools.partial(kernel, n, factor), out_shape=jax.ShapeD...]
    dot_general x12 -> x0, matrix products: 23.5 us -> none  [the longest x4 12.4 us: kernel_tile(): inner = jnp.dot(points, block, preferred_element_type=jnp.float32)]
    reduce_sum x2 -> x0, other arithmetic: 5.41 us -> none  [the longest x1 4.5 us: kernel_tile(): sq_centers = jnp.sum(jnp.square(block.astype(jnp.float32)), axis=0)]
    psum x1 -> x0, blocking collectives: 5.02 us -> none  [on_device(): tangent = lax.psum(tangent, 'ctr')]
  transfers between devices with their start and end apart: 3 -> 0, of which waited for: 3 -> 0; matrix products, arithmetic and copies ran while one was open for 6% -> 0% of each run, Pallas kernels for 0% -> 0%
where the time goes in v2:
time: 33.4 us; the launch traced here: 32.8 us
  Pallas kernels  30.9 us (93%)
  local copies, waits for them, and re-layouts  1.87 us (6%)
    pallas_call x1, Pallas kernels, on_device(): pl.pallas_call(functools.partial(kernel, n, factor), out_shape=jax.ShapeD...  30.9 us
    unnamed x1, local copies, waits for them, and re-layouts  1.87 us

profile of v2, /device:TPU:1, one launch (start us, length us, event | category | flops | bytes accessed | tf_op | source)
XLA Modules:
  0.0 32.8 jit_solution(6107643688003222888)
XLA Ops:
  0.0 30.9 %shard_map.46 = f32[32,4096]{1,0:T(8,128)} custom-call(bf16[192,128]{1,0:T(8,128)(2,1)} %points_in.1, bf16[32,192]{1,0:T(8,128)(2,1)} %bitcast.1, bf16[128,4096]{1,0:T(8,128)(2,1)} %centers_in.1, bf16[32,4096]{1,0:T(8,128)(2,1)} %coef_in.1), custom_call_target="tpu_custom_call" | custom-call | tf_op jit(solution)/shard_map/pallas_call | solution.py:250
  31.0 1.9 %copy.6 = f32[32,4096]{1,0:T(8,128)} copy(f32[32,4096]{1,0:T(8,128)} %shard_map.46) | data formatting | bytes 1048576

commit v3 on v2

--- a/solution.py
+++ b/solution.py
@@ -37,6 +37,7 @@
     wide = mine.shape[2]
     chunks = total // wide
     pairs = n // 2
+    broad = min(1024, total)
     sibling = {"ctr": 1 - c}
 
     def peer(s):
@@ -125,11 +126,11 @@
         return jnp.concatenate([block, extra.astype(BF16)], axis=1)
 
     def pair(i, left, side):
-        for start in range(0, total, wide):
+        for start in range(0, total, broad):
             inner = jnp.dot(
-                left, aug[side, :, start : start + wide], preferred_element_type=F32
+                left, aug[side, :, start : start + broad], preferred_element_type=F32
             )
-            tile[i, side, :, start : start + wide] = jnp.exp2(inner * factor).astype(BF16)
+            tile[i, side, :, start : start + broad] = jnp.exp2(inner * factor).astype(BF16)
         return jnp.dot(tile[i, side], turned[side], preferred_element_type=F32)
 
     def keep(i, value):
@@ -245,7 +246,7 @@
         labels, total = coef.shape
         factor = 2.0 * (32.0 / depth) * math.log2(math.e)
         half = rows // 2
-        wide = min(512, total)
+        wide = min(2048, total)
         dma = pltpu.SemaphoreType.DMA
         return pl.pallas_call(
             functools.partial(kernel, n, factor),

time: 33.4 us -> 31 us (0.928); the launches traced: 32.8 us -> 30.8 us
  Pallas kernels: 30.9 us -> 28.9 us
    pallas_call x1, Pallas kernels: 30.9 us -> 28.9 us  [on_device(): pl.pallas_call(functools.partial(kernel, n, factor), out_shape=jax.ShapeD...]
where the time goes in v3:
time: 31 us; the launch traced here: 30.8 us
  Pallas kernels  28.9 us (93%)
  local copies, waits for them, and re-layouts  1.87 us (6%)
    pallas_call x1, Pallas kernels, on_device(): pl.pallas_call(functools.partial(kernel, n, factor), out_shape=jax.ShapeD...  28.9 us
    unnamed x1, local copies, waits for them, and re-layouts  1.87 us

profile of v3, /device:TPU:1, one launch (start us, length us, event | category | flops | bytes accessed | tf_op | source)
XLA Modules:
  0.0 30.8 jit_solution(11486789703514282748)
XLA Ops:
  0.0 28.9 %shard_map.46 = f32[32,4096]{1,0:T(8,128)} custom-call(bf16[192,128]{1,0:T(8,128)(2,1)} %points_in.1, bf16[32,192]{1,0:T(8,128)(2,1)} %bitcast.1, bf16[128,4096]{1,0:T(8,128)(2,1)} %centers_in.1, bf16[32,4096]{1,0:T(8,128)(2,1)} %coef_in.1), custom_call_target="tpu_custom_call" | custom-call | tf_op jit(solution)/shard_map/pallas_call | solution.py:251
  29.0 1.9 %copy.6 = f32[32,4096]{1,0:T(8,128)} copy(f32[32,4096]{1,0:T(8,128)} %shard_map.46) | data formatting | bytes 1048576
